TPU v7x, 32 devices: a whole 2x2x4 slice. The times are simulated.
32 devices in a mesh: groups: 2 (over y), panel: 4 (over z), layer: 2 (over x), sub: 2 (over core).
Axes of the slice: x: 2, y: 2, z: 4, core: 2. Of those that a mesh axis runs over, the one named last changes fastest.
Arguments:
- values: float32 [32, 8, 128, 128], P(('groups', 'panel', 'sub'), 'layer'), parts along dimension 0, may hold values from -1 to 1
- columns: int32 [32, 8], P(('groups', 'panel', 'sub'), 'layer'), parts along dimension 0, may hold values from 0 to 15, as said below
Outputs:
- purified: float32 [32, 8, 128, 128], P(('groups', 'panel', 'sub'), 'layer'), parts along dimension 0
There are 2 independent parts, one for each index of `groups`. A program takes and returns all parts, laid end to end along the dimension named above; each array names one. Nothing has to cross between parts.
Inputs may be any that keep to these rules, and one draw needn't show every extreme that they name: Each block row names 8 different block columns; slot 0 of block row i names column i.
All inputs are finite; a program needn't handle non-finite values.
Results may differ from a plain program's by a relative error of at most 0.0003.
Values sent between devices are 32-bit elements; how exact they have to be, the bound alone decides.
A program may use at most 128 MiB of HBM per device.

v0:
```python
import jax
import jax.numpy as jnp
from jax import lax
from jax.sharding import PartitionSpec as P

highest_precision = lax.Precision.HIGHEST


def masked_rows(left_vals, left_cols, right_vals, right_cols):
    block_products = jnp.einsum(
        "ruab,rusbc->rusac", left_vals, right_vals, precision=highest_precision
    )
    target_blocks = (left_cols[:, :, None, None] == right_cols[:, None, :, :]).astype(jnp.float32)
    return jnp.einsum(
        "rtus,rusac->rtac", target_blocks, block_products, precision=highest_precision
    )


def shards(values, columns):
    full_vals, full_cols = (
        lax.all_gather(values, "layer", axis=1, tiled=True),
        lax.all_gather(columns, "layer", axis=1, tiled=True),
    )
    slot_dev = values.shape[1]
    start_vals = jnp.zeros(full_cols.shape + values.shape[1:], jnp.float32)
    start_cols = jnp.zeros(full_cols.shape + (slot_dev,), jnp.int32)
    slab_pieces = (
        lax.all_gather(values, ("panel", "sub"), axis=0, tiled=True),
        lax.all_gather(columns, ("panel", "sub"), axis=0, tiled=True),
    )
    count = slab_pieces[0].shape[0]
    block_offset = full_cols - jnp.int32(0)
    inside = (block_offset >= 0) & (block_offset < count)
    clipped = jnp.clip(block_offset, 0, count - 1)
    picked_vals = slab_pieces[0][clipped]
    picked_cols = slab_pieces[1][clipped]
    kept_vals = jnp.where(inside[:, :, None, None, None], picked_vals, start_vals)
    kept_cols = jnp.where(inside[:, :, None], picked_cols, start_cols)
    square_part = masked_rows(full_vals, full_cols, kept_vals, kept_cols)
    square_own = lax.psum_scatter(square_part, "layer", scatter_dimension=1, tiled=True)
    square_full = lax.all_gather(square_own, "layer", axis=1, tiled=True)
    cube_part = masked_rows(square_full, full_cols, kept_vals, kept_cols)
    cube_own = lax.psum_scatter(cube_part, "layer", scatter_dimension=1, tiled=True)
    return 3.0 * square_own - 2.0 * cube_own


def solution(mesh):
    return jax.shard_map(
        shards,
        mesh=mesh,
        in_specs=(
            P(("groups", "panel", "sub"), "layer", None, None),
            P(("groups", "panel", "sub"), "layer"),
        ),
        out_specs=P(("groups", "panel", "sub"), "layer", None, None),
        check_vma=False,
    )
```

profile of v0, /device:TPU:0, one launch (start us, length us, event | category | flops | bytes accessed | tf_op | source)
XLA Modules:
  0.0 200.0 jit_solution(14259342733175774524)
XLA Ops:
  6.5 0.0 all-gather.6.cloned.1.call-start
  6.5 0.7 all-gather.6.cloned.1.call-update
  7.3 0.0 all-gather.8.cloned.1.call-start
  7.3 0.7 all-gather.8.cloned.1.call-update
  8.0 0.0 reduce-scatter.3.cloned.1.call-start
  8.1 5.4 %all-gather = s32[2,4,2]{1,2,0:T(2,128)S(1)} all-gather(s32[1,4,2]{1,2,0:T(2,128)} %bitcast.50), channel_id=1, replica_groups=mesh['groups'=2,'panel'=4,'layer'=2,'sub'=2] {'layer'}, dimensions={0}, use_global_device_ids=true | all-gather | bytes 96 | tf_op jit(solution)/shard_map/all_gather | solution.py:22
  13.5 0.1 reshape.27
  13.6 0.1 reshape.8
  13.7 12.7 %all-gather.1 = s32[8,2,4]{2,1,0:T(2,128)S(1)} all-gather(s32[1,2,4]{2,1,0:T(2,128)} %bitcast.51), channel_id=1, replica_groups=mesh['groups'=2,'panel'=4,'layer'=2,'sub'=2] {'panel','sub'}, dimensions={0}, use_global_device_ids=true | all-gather | bytes 288 | tf_op jit(solution)/shard_map/all_gather | solution.py:29
  26.4 0.6 gather_fusion
  26.9 0.1 copy.20
  27.0 31.8 %all-gather.6.cloned.1.call-done = f32[16,4,128,128]{3,2,1,0:T(8,128)} async-done(((f32[2,4,128,128]{3,2,1,0:T(8,128)}), f32[16,4,128,128]{3,2,1,0:T(8,128)}) %all-gather.6.cloned.1.call-update) | async-done | bytes 4194320 | tf_op jit(solution)/shard_map/all_gather | solution.py:28
  58.8 4.9 %gather_fusion.1 = f32[16,4,128,128]{3,2,1,0:T(8,128)} fusion(f32[16,4,128,128]{3,2,1,0:T(8,128)} %all-gather.6.cloned.1.call-done, s32[1024]{0:T(1024)S(1)} %pad_clamp_fusion), kind=kCustom, calls=%fused_computation.1 | custom fusion | bytes 8388672 | tf_op jit(solution)/shard_map/gather | solution.py:35
  63.8 16.8 %all-gather.8.cloned.1.call-done = f32[2,8,128,128]{3,2,1,0:T(8,128)} async-done(((f32[2,4,128,128]{3,2,1,0:T(8,128)}), f32[2,8,128,128]{3,2,1,0:T(8,128)}) %all-gather.8.cloned.1.call-update) | async-done | bytes 1048592 | tf_op jit(solution)/shard_map/all_gather | solution.py:21
  80.5 10.9 %fusion.6 = f32[2,8,4,128,128]{4,3,2,1,0:T(8,128)} fusion(f32[2,8,4,128,128]{4,3,2,1,0:T(8,128)} %bitcast.44, pred[2,8]{1,0:T(4,128)(4,1)S(1)} %compare_and_fusion, f32[2,8,128,128]{3,2,1,0:T(8,128)} %all-gather.8.cloned.1.call-done), kind=kOutput, calls=%fused_computation.8 | convolution fusion | flops 1611661312 | bytes 9437200 | tf_op jit(solution)/shard_map/ruab,rusbc->rusac/dot_general | solution.py:10
  91.4 5.4 %copy.14 = f32[2,8,4,128,128]{3,1,2,4,0:T(8,128)} copy(f32[2,8,4,128,128]{4,3,2,1,0:T(8,128)} %fusion.6) | data formatting | bytes 8388608 | tf_op jit(solution)/shard_map/ruab,rusbc->rusac/dot_general | solution.py:10
  96.9 6.0 %fusion.12 = f32[2,8,128,128]{3,1,2,0:T(8,128)S(1)} fusion(f32[2,8,4,128,128]{3,1,2,4,0:T(8,128)} %copy.14, s32[2,8,4]{1,2,0:T(4,128)S(1)} %copy.9, s32[2,8]{1,0:T(2,128)S(1)} %bitcast.48), kind=kOutput, calls=%fused_computation.14 | convolution fusion | flops 100663808 | bytes 5243200 | tf_op jit(solution)/shard_map/rtus,rusac->rtac/dot_general | solution.py:14
  102.9 1.2 copy.10
  104.1 0.0 reduce-scatter.3.cloned.1.call-update
  104.1 0.0 all-gather.10.cloned.1.call-start
  104.1 20.4 %reduce-scatter.3.cloned.1.call-done = f32[2,4,128,128]{3,2,0,1:T(8,128)} async-done(((f32[2,8,128,128]{3,2,0,1:T(8,128)}), f32[2,4,128,128]{3,2,0,1:T(8,128)}) %reduce-scatter.3.cloned.1.call-update) | async-done | bytes 524304 | tf_op jit(solution)/shard_map/reduce_scatter | solution.py:40
  124.6 0.0 all-gather.10.cloned.1.call-update
  124.6 0.2 reduce-scatter.5.cloned.1.call-start
  124.8 22.6 %all-gather.10.cloned.1.call-done = f32[2,8,128,128]{3,2,0,1:T(8,128)} async-done(((f32[2,4,128,128]{3,2,0,1:T(8,128)}), f32[2,8,128,128]{3,2,0,1:T(8,128)}) %all-gather.10.cloned.1.call-update) | async-done | bytes 1048592 | tf_op jit(solution)/shard_map/all_gather | solution.py:41
  147.4 10.9 %fusion.4 = f32[2,8,4,128,128]{4,3,2,1,0:T(8,128)} fusion(f32[2,8,4,128,128]{4,3,2,1,0:T(8,128)} %bitcast.45, pred[2,8]{1,0:T(4,128)(4,1)S(1)} %compare_and_fusion, f32[2,8,128,128]{3,2,0,1:T(8,128)} %all-gather.10.cloned.1.call-done), kind=kOutput, calls=%fused_computation.6 | convolution fusion | flops 1611661312 | bytes 9437200 | tf_op jit(solution)/shard_map/ruab,rusbc->rusac/dot_general | solution.py:10
  158.3 5.5 %copy.18 = f32[2,8,4,128,128]{3,1,2,4,0:T(8,128)} copy(f32[2,8,4,128,128]{4,3,2,1,0:T(8,128)} %fusion.4) | data formatting | bytes 8388608 | tf_op jit(solution)/shard_map/ruab,rusbc->rusac/dot_general | solution.py:10
  163.8 0.0 copy-start
  163.8 6.1 %fusion.15 = f32[2,8,128,128]{3,1,2,0:T(8,128)S(1)} fusion(f32[2,8,4,128,128]{3,1,2,4,0:T(8,128)} %copy.18, s32[2,8,4]{1,2,0:T(4,128)S(1)} %copy.9, s32[2,8]{1,0:T(2,128)S(1)} %bitcast.49), kind=kOutput, calls=%fused_computation.15 | convolution fusion | flops 100663808 | bytes 5243200 | tf_op jit(solution)/shard_map/rtus,rusac->rtac/dot_general | solution.py:14
  169.8 1.2 copy.11
  171.0 0.0 reduce-scatter.5.cloned.1.call-update
  171.0 20.5 %reduce-scatter.5.cloned.1.call-done = f32[2,4,128,128]{3,2,0,1:T(8,128)} async-done(((f32[2,8,128,128]{3,2,0,1:T(8,128)}), f32[2,4,128,128]{3,2,0,1:T(8,128)}) %reduce-scatter.5.cloned.1.call-update) | async-done | bytes 524304 | tf_op jit(solution)/shard_map/reduce_scatter | solution.py:43
  191.5 0.0 copy-done
  191.5 1.1 multiply_subtract_fusion
  192.6 0.8 copy.12
  (6 shorter events, 0.0 us)
Async XLA Ops:
  6.5 52.3 %all-gather.6.cloned.1.call-start = ((), (), s32[]{:S(2)}) async-start(), calls=%async_computation.2 | async-start | bytes 4718592 | tf_op jit(solution)/shard_map/all_gather | solution.py:28
  7.3 73.3 %all-gather.8.cloned.1.call-start = ((), (), s32[]{:S(2)}) async-start(), calls=%async_computation.3 | async-start | bytes 1572864 | tf_op jit(solution)/shard_map/all_gather | solution.py:21
  8.0 116.6 %reduce-scatter.3.cloned.1.call-start = ((), (), s32[]{:S(2)}) async-start(), calls=%async_computation.4 | async-start | bytes 1572864 | tf_op jit(solution)/shard_map/reduce_scatter | solution.py:40
  104.1 43.3 %all-gather.10.cloned.1.call-start = ((), (), s32[]{:S(2)}) async-start(), calls=%async_computation.5 | async-start | bytes 1572864 | tf_op jit(solution)/shard_map/all_gather | solution.py:41
  124.6 66.9 %reduce-scatter.5.cloned.1.call-start = ((), (), s32[]{:S(2)}) async-start(), calls=%async_computation.6 | async-start | bytes 1572864 | tf_op jit(solution)/shard_map/reduce_scatter | solution.py:43
  163.8 27.7 %copy-start = (f32[2,4,128,128]{3,2,0,1:T(8,128)S(1)}, f32[2,4,128,128]{3,2,0,1:T(8,128)}, u32[]{:S(2)}) copy-start(f32[2,4,128,128]{3,2,0,1:T(8,128)} %reduce-scatter.3.cloned.1.call-done) | copy-start | bytes 1572868
Sparse Core Ops, SparseCore 0:
  9.0 49.8 all-gather.5
  60.4 20.1 all-gather.7
  104.2 20.3 reduce-scatter.2
  126.0 21.2 all-gather.9
  171.2 20.3 reduce-scatter.4
where the time goes:
time: 200 us
  waiting for transfers between devices  113 us (56%)
  matrix products  33.9 us (17%)
  local copies, waits for them, and re-layouts  19.9 us (10%)
  blocking collectives  18.1 us (9%)
  between operations  13.2 us (7%)
    all_gather x1, waiting for transfers between devices, shards(): lax.all_gather(values, ('panel', 'sub'), axis=0, tiled=True)  31.8 us
    all_gather x1, waiting for transfers between devices, shards(): square_full = lax.all_gather(square_own, 'layer', axis=1, tiled=True)  22.6 us
    dot_general x2, matrix products, masked_rows(): jnp.einsum('ruab,rusbc->rusac', left_vals, right_vals, precision=highest_...  21.8 us
    reduce_scatter x1, waiting for transfers between devices, shards(): lax.psum_scatter(cube_part, 'layer', scatter_dimension=1, tiled=True)  20.5 us
    reduce_scatter x1, waiting for transfers between devices, shards(): lax.psum_scatter(square_part, 'layer', scatter_dimension=1, tiled=True)  20.4 us
    all_gather x1, waiting for transfers between devices, shards(): lax.all_gather(values, 'layer', axis=1, tiled=True)  16.8 us
    all_gather x1, blocking collectives, shards(): lax.all_gather(columns, ('panel', 'sub'), axis=0, tiled=True)  12.7 us
    dot_general x2, matrix products, masked_rows(): jnp.einsum('rtus,rusac->rtac', target_blocks, block_products, precision=h...  12.1 us
  transfers between devices with their start and end apart: 5, of which 5 were waited for; matrix products, arithmetic and copies ran while one was open for 3% of the time, Pallas kernels for 0%

commit v1 on v0

v1 whole, which is shorter than its diff:
```python
import jax
import jax.numpy as jnp
from jax import lax
from jax.experimental import pallas as pl
from jax.experimental.pallas import tpu as pltpu
from jax.sharding import PartitionSpec as P

highest_precision = lax.Precision.HIGHEST
MESH = pl.DeviceIdType.MESH


def masked_rows(left_vals, left_cols, right_vals, right_cols):
    block_products = jnp.einsum(
        "ruab,rusbc->rusac", left_vals, right_vals, precision=highest_precision
    )
    target_blocks = (left_cols[:, :, None, None] == right_cols[:, None, :, :]).astype(jnp.float32)
    return jnp.einsum(
        "rtus,rusac->rtac", target_blocks, block_products, precision=highest_precision
    )


def shards_general(values, columns):
    full_vals, full_cols = (
        lax.all_gather(values, "layer", axis=1, tiled=True),
        lax.all_gather(columns, "layer", axis=1, tiled=True),
    )
    slab_pieces = (
        lax.all_gather(values, ("panel", "sub"), axis=0, tiled=True),
        lax.all_gather(columns, ("panel", "sub"), axis=0, tiled=True),
    )
    kept_vals = slab_pieces[0][full_cols]
    kept_cols = slab_pieces[1][full_cols]
    square_part = masked_rows(full_vals, full_cols, kept_vals, kept_cols)
    square_own = lax.psum_scatter(square_part, "layer", scatter_dimension=1, tiled=True)
    square_full = lax.all_gather(square_own, "layer", axis=1, tiled=True)
    cube_part = masked_rows(square_full, full_cols, kept_vals, kept_cols)
    cube_own = lax.psum_scatter(cube_part, "layer", scatter_dimension=1, tiled=True)
    return 3.0 * square_own - 2.0 * cube_own


def kernel(tile_ref, v_ref, o_ref, xbuf, hi, lo, sq, tq, tz, tabs,
           send_sem, recv_own, recv_sib, tsend, trecv, local_sem):
    z = lax.axis_index("panel")
    x = lax.axis_index("layer")
    c = lax.axis_index("sub")
    xo, co = 1 - x, 1 - c
    rows, half, blk, _ = v_ref.shape
    slots = 2 * half
    zero_block = hi.shape[0] - 1

    far = z // 2
    zm = z + far * (3 - 2 * z)
    is_end = zm == 0
    is_mid = zm == 1

    def plane(q):
        return q + far * (3 - 2 * q)

    q_list = [plane(zm), plane(1 - zm), plane(2), plane(3)]
    z_out = plane(jnp.maximum(zm - 1, 0))
    z_in = plane(zm + 1)

    barrier = pltpu.get_barrier_semaphore()
    others = [lax.rem(z + d, 4) for d in (1, 2, 3)]
    for dev in ({"sub": co}, {"layer": xo}, *({"panel": zz} for zz in others)):
        pl.semaphore_signal(barrier, inc=1, device_id=dev, device_id_type=MESH)
    pl.semaphore_wait(barrier, 5)

    def piece(zz, xx, cc, r):
        return xbuf.at[(zz * 2 + cc) * rows + r, pl.ds(xx * half, half)]

    def number(zz, xx, r):
        return (zz * 2 + xx) * rows + r

    sends = []

    def send(pred, src, zz, xx, r, dev, sib=False):
        slot = len(sends)
        recv = recv_sib if sib else recv_own
        copy = pltpu.make_async_remote_copy(
            src_ref=src,
            dst_ref=piece(zz, xx, c, r),
            send_sem=send_sem.at[slot],
            recv_sem=recv.at[number(zz, xx, r)],
            device_id=dev,
            device_id_type=MESH,
        )
        sends.append((pred, copy))
        if pred is None:
            copy.start()
        else:
            pl.when(pred)(copy.start)

    def wait_piece(zz, xx, cc, r, sem):
        dst = piece(zz, xx, cc, r)
        pltpu.make_async_remote_copy(
            src_ref=dst, dst_ref=dst, send_sem=send_sem.at[0],
            recv_sem=sem.at[number(zz, xx, r)],
            device_id={"sub": co}, device_id_type=MESH,
        ).wait_recv()

    def small(src, dst, s, r, dev):
        return pltpu.make_async_remote_copy(
            src_ref=src, dst_ref=dst, send_sem=tsend.at[s], recv_sem=trecv.at[r],
            device_id=dev, device_id_type=MESH,
        )

    tq[x, c] = tile_ref[...]
    t1 = small(tq.at[x, c], tq.at[x, c], 0, 0, {"sub": co})
    t1.start()

    for r in range(rows):
        own = v_ref.at[r]
        send(None, own, z, x, r, {"panel": z_in})
        send(is_mid, own, z, x, r, {"panel": z_out})
        send(None, own, z, x, r, {"layer": xo})
        send(None, own, z, x, r, {"sub": co}, sib=True)

    t1.wait_recv()
    t2 = small(tq.at[x], tq.at[x], 1, 1, {"layer": xo})
    t2.start()

    for r in range(rows):
        xbuf[(z * 2 + c) * rows + r, pl.ds(x * half, half)] = v_ref[r]
    hi[zero_block] = jnp.zeros((blk, blk), jnp.bfloat16)
    lo[zero_block] = jnp.zeros((blk, blk), jnp.bfloat16)
    sq[...] = jnp.zeros_like(sq)

    t2.wait_recv()
    tz[z] = tq[0] + tq[1]
    t3 = [
        small(tz.at[z], tz.at[z], 2 + d, 2 + z, {"panel": others[d]}) for d in range(3)
    ]
    for t in t3:
        t.start()

    def arrive(q, other, r):
        zz = q_list[q]
        if not other:
            wait_piece(zz, x, c, r, recv_own)
            src = piece(zz, x, c, r)
            if q == 1:
                send(is_mid, src, zz, x, r, {"panel": z_in})
                if r == 0:
                    send(is_end, src, zz, x, r, {"layer": xo})
            else:
                send(is_mid, src, zz, x, r, {"panel": z_out})
                send(None, src, zz, x, r, {"layer": xo})
            send(None, src, zz, x, r, {"sub": co}, sib=True)
        else:
            wait_piece(zz, xo, c, r, recv_own)
            src = piece(zz, xo, c, r)
            if q == 0:
                send(is_end, src, zz, xo, r, {"panel": z_in})
            send(None, src, zz, xo, r, {"sub": co}, sib=True)

    def late_extra():
        r = rows - 1
        send(is_mid, piece(z, xo, c, r), z, xo, r, {"panel": z_out})

    def convert(row):
        val = xbuf[row]
        top = val.astype(jnp.bfloat16)
        hi[pl.ds(row * slots, slots)] = top
        lo[pl.ds(row * slots, slots)] = (val - top.astype(jnp.float32)).astype(jnp.bfloat16)

    def block_at(zz, cc, r, col):
        found = tabs[zz, cc, r, col]
        row = (zz * 2 + cc) * rows + r
        return jnp.where(found > 0, row * slots + found - 1, zero_block)

    def chunk_ready(q, r):
        zz = q_list[q]
        for xx in (x, xo):
            wait_piece(zz, xx, co, r, recv_sib)
        for cc in range(2):
            convert((zz * 2 + cc) * rows + r)

    def times(lh, ll, wh, wl):
        m = lh.shape[0]
        both = jnp.dot(jnp.concatenate([lh, ll], axis=0), wh, preferred_element_type=jnp.float32)
        return both[:m] + both[m:] + jnp.dot(lh, wl, preferred_element_type=jnp.float32)

    def chunk(q, r):
        zz = q_list[q]

        def one_row(i, carry):
            lidx = [block_at(z, c, i, (zz * 2 + cc) * rows + r) for cc in range(2)]
            lh = jnp.concatenate([hi[n] for n in lidx], axis=1)
            ll = jnp.concatenate([lo[n] for n in lidx], axis=1)
            for tp in range(slots // 2):
                ridx = [
                    [block_at(zz, cc, r, tabs[z, c, 2 + i, 2 * tp + e]) for cc in range(2)]
                    for e in range(2)
                ]
                wh = jnp.concatenate(
                    [jnp.concatenate([hi[n] for n in col], axis=0) for col in ridx], axis=1)
                wl = jnp.concatenate(
                    [jnp.concatenate([lo[n] for n in col], axis=0) for col in ridx], axis=1)
                sq[i, tp] += times(lh, ll, wh, wl)
            return carry

        lax.fori_loop(0, rows, one_row, 0)

    arrive(1, False, 0)
    arrive(0, True, 0)
    arrive(1, False, 1)
    arrive(0, True, 1)
    for zz, s in zip(others, range(3)):
        small(tz.at[zz], tz.at[zz], 2, 2 + zz, {"sub": co}).wait_recv()
    stage = pltpu.make_async_copy(tz, tabs, local_sem)
    stage.start()
    chunk_ready(0, 0)
    chunk_ready(0, 1)
    stage.wait()
    chunk(0, 0)
    arrive(2, False, 0)
    arrive(2, False, 1)
    chunk(0, 1)
    arrive(1, True, 0)
    chunk_ready(1, 0)
    chunk(1, 0)
    arrive(2, True, 0)
    chunk_ready(2, 0)
    arrive(3, False, 0)
    chunk(2, 0)
    arrive(2, True, 1)
    chunk_ready(2, 1)
    arrive(3, False, 1)
    late_extra()
    chunk(2, 1)
    arrive(3, True, 0)
    chunk_ready(3, 0)
    chunk(3, 0)
    arrive(3, True, 1)
    arrive(1, True, 1)
    chunk_ready(3, 1)
    chunk(3, 1)
    chunk_ready(1, 1)
    chunk(1, 1)

    def cube_row(i, carry):
        full = jnp.concatenate([sq[i, tp] for tp in range(slots // 2)], axis=1)
        sh = full.astype(jnp.bfloat16)
        sl = (full - sh.astype(jnp.float32)).astype(jnp.bfloat16)
        ks = [tabs[z, c, 2 + i, u] for u in range(slots)]
        for e in range(half // 2):
            cols = [tabs[z, c, 2 + i, x * half + 2 * e + f] for f in range(2)]
            idx = []
            for col in cols:
                one = []
                for k in ks:
                    found = tabs[k // (2 * rows), (k // rows) % 2, k % rows, col]
                    one.append(jnp.where(found > 0, k * slots + found - 1, zero_block))
                idx.append(one)
            wh = jnp.concatenate(
                [jnp.concatenate([hi[n] for n in one], axis=0) for one in idx], axis=1)
            wl = jnp.concatenate(
                [jnp.concatenate([lo[n] for n in one], axis=0) for one in idx], axis=1)
            res = 3.0 * sq[i, x * (half // 2) + e] - 2.0 * times(sh, sl, wh, wl)
            o_ref[i, 2 * e] = res[:, :blk]
            o_ref[i, 2 * e + 1] = res[:, blk:]
        return carry

    lax.fori_loop(0, rows, cube_row, 0)

    for t in (t1, t2, *t3):
        t.wait_send()
    for pred, copy in sends:
        if pred is None:
            copy.wait_send()
        else:
            pl.when(pred)(copy.wait_send)


def shards_kernel(values, columns):
    rows, half, blk, _ = values.shape
    slots, nb = 2 * half, 8 * rows
    x = lax.axis_index("layer")
    lanes = jnp.arange(128, dtype=jnp.int32)
    place = jnp.arange(half, dtype=jnp.int32) + x * half
    by_col = jnp.sum(
        jnp.where(columns[:, :, None] == lanes, place[None, :, None] + 1, 0), axis=1)
    by_slot = jnp.sum(
        jnp.where(place[None, :, None] == lanes, columns[:, :, None], 0), axis=1)
    tile = jnp.concatenate(
        [by_col, by_slot, jnp.zeros((8 - 2 * rows, 128), jnp.int32)], axis=0).astype(jnp.int32)
    vmem = pl.BlockSpec(memory_space=pltpu.VMEM)
    return pl.pallas_call(
        kernel,
        out_shape=jax.ShapeDtypeStruct(values.shape, jnp.float32),
        in_specs=[vmem, vmem],
        out_specs=vmem,
        scratch_shapes=[
            pltpu.VMEM((nb, slots, blk, blk), jnp.float32),
            pltpu.VMEM((nb * slots + 1, blk, blk), jnp.bfloat16),
            pltpu.VMEM((nb * slots + 1, blk, blk), jnp.bfloat16),
            pltpu.VMEM((rows, slots // 2, blk, 2 * blk), jnp.float32),
            pltpu.VMEM((2, 2, 8, 128), jnp.int32),
            pltpu.VMEM((4, 2, 8, 128), jnp.int32),
            pltpu.SMEM((4, 2, 8, 128), jnp.int32),
            pltpu.SemaphoreType.DMA((36,)),
            pltpu.SemaphoreType.DMA((4 * 2 * rows,)),
            pltpu.SemaphoreType.DMA((4 * 2 * rows,)),
            pltpu.SemaphoreType.DMA((5,)),
            pltpu.SemaphoreType.DMA((6,)),
            pltpu.SemaphoreType.DMA,
        ],
        compiler_params=pltpu.CompilerParams(
            collective_id=0, has_side_effects=True, vmem_limit_bytes=48 * 1024 * 1024,
        ),
        cost_estimate=pl.CostEstimate(
            flops=3 * 2 * 3 * 64 * 2 * blk ** 3, bytes_accessed=2 * values.size * 4,
            transcendentals=0),
    )(tile, values)


def solution(mesh):
    shape = dict(mesh.shape)

    def shards(values, columns):
        fits = (shape["panel"], shape["layer"], shape["sub"]) == (4, 2, 2)
        if fits and values.shape == (2, 4, 128, 128):
            return shards_kernel(values, columns)
        return shards_general(values, columns)

    return jax.shard_map(
        shards,
        mesh=mesh,
        in_specs=(
            P(("groups", "panel", "sub"), "layer", None, None),
            P(("groups", "panel", "sub"), "layer"),
        ),
        out_specs=P(("groups", "panel", "sub"), "layer", None, None),
        check_vma=False,
    )
```

time: 200 us -> 60.8 us (0.30)
  waiting for transfers between devices: 113 us -> 0 us
  Pallas kernels: 0 us -> 57.9 us
  matrix products: 33.9 us -> 0 us
  blocking collectives: 18.1 us -> 0 us
  local copies, waits for them, and re-layouts: 19.9 us -> 2.52 us
  between operations: 13.2 us -> 0.01 us
    all_gather x3 -> x0, waiting for transfers between devices: 71.1 us -> none  [the longest x1 31.8 us: shards(): lax.all_gather(values, ('panel', 'sub'), axis=0, tiled=True)]
    pallas_call x0 -> x1, Pallas kernels: none -> 57.9 us  [shards_kernel(): pl.pallas_call(kernel, out_shape=jax.ShapeDtypeStruct(values.shape, jnp.f...]
    reduce_scatter x2 -> x0, waiting for transfers between devices: 40.9 us -> none  [the longest x1 20.5 us: shards(): lax.psum_scatter(cube_part, 'layer', scatter_dimension=1, tiled=True)]
    dot_general x4 -> x0, matrix products: 33.9 us -> none  [the longest x2 21.8 us: masked_rows(): jnp.einsum('ruab,rusbc->rusac', left_vals, right_vals, precision=highest_...]
    all_gather x2 -> x0, blocking collectives: 18.1 us -> none  [the longest x1 12.7 us: shards(): lax.all_gather(columns, ('panel', 'sub'), axis=0, tiled=True)]
    dot_general x4 -> x0, local copies, waits for them, and re-layouts: 13.3 us -> none  [the longest x2 10.9 us: masked_rows(): jnp.einsum('ruab,rusbc->rusac', left_vals, right_vals, precision=highest_...]
    gather x3 -> x0, local copies, waits for them, and re-layouts: 5.6 us -> none  [the longest x1 4.95 us: shards(): picked_vals = slab_pieces[0][clipped]]
    unnamed x3 -> x5, local copies, waits for them, and re-layouts: 0.09 us -> 2.44 us
  transfers between devices with their start and end apart: 5 -> 0, of which waited for: 5 -> 0; matrix products, arithmetic and copies ran while one was open for 3% -> 0% of each run, Pallas kernels for 0% -> 0%
where the time goes in v1:
time: 60.8 us; the launch traced here: 60.7 us
  Pallas kernels  57.9 us (95%)
  local copies, waits for them, and re-layouts  2.52 us (4%)
    pallas_call x1, Pallas kernels, shards_kernel(): pl.pallas_call(kernel, out_shape=jax.ShapeDtypeStruct(values.shape, jnp.f...  57.9 us
    unnamed x5, local copies, waits for them, and re-layouts  2.44 us

profile of v1, /device:TPU:0, one launch (start us, length us, event | category | flops | bytes accessed | tf_op | source)
XLA Modules:
  0.0 60.7 jit_solution(3130971464741967022)
XLA Ops:
  0.0 0.1 pad.2.clone
  0.1 0.0 copy-start.1
  0.1 0.1 iota_compare_fusion.1
  0.2 0.6 copy-done.1
  0.8 0.1 select_reduce_fusion.1
  0.9 0.1 add_add_fusion.tile_ref
  0.9 0.0 copy-start
  0.9 1.0 %copy-done = f32[2,4,128,128]{3,2,1,0:T(8,128)S(1)} copy-done((f32[2,4,128,128]{3,2,1,0:T(8,128)S(1)}, f32[2,4,128,128]{3,2,1,0:T(8,128)}, u32[]{:S(2)}) %copy-start) | copy-done | bytes 524312
  2.0 57.9 %shard_map.28 = f32[2,4,128,128]{3,2,1,0:T(8,128)S(1)} custom-call(s32[8,128]{1,0:T(8,128)S(1)} %add_add_fusion.tile_ref, f32[2,4,128,128]{3,2,1,0:T(8,128)S(1)} %copy-done), custom_call_target="tpu_custom_call" | custom-call | flops 4831838208 | bytes 1048576 | tf_op jit(solution)/shard_map/pallas_call | solution.py:289
  59.9 0.8 %copy.4 = f32[2,4,128,128]{3,2,1,0:T(8,128)} copy(f32[2,4,128,128]{3,2,1,0:T(8,128)S(1)} %shard_map.28) | data formatting | bytes 1048576
  (2 shorter events, 0.0 us)
Async XLA Ops:
  0.1 0.7 %copy-start.1 = (s32[2,4]{1,0:T(2,128)S(1)}, s32[2,4]{1,0:T(2,128)}, u32[]{:S(2)}) copy-start(s32[2,4]{1,0:T(2,128)} %param.3) | copy-start | bytes 100
  0.9 1.0 %copy-start = (f32[2,4,128,128]{3,2,1,0:T(8,128)S(1)}, f32[2,4,128,128]{3,2,1,0:T(8,128)}, u32[]{:S(2)}) copy-start(f32[2,4,128,128]{3,2,1,0:T(8,128)} %v_ref.1) | copy-start | bytes 1572868

commit v2 on v1

--- a/solution.py
+++ b/solution.py
@@ -38,14 +38,15 @@
     return 3.0 * square_own - 2.0 * cube_own
 
 
-def kernel(tile_ref, v_ref, o_ref, xbuf, hi, lo, sq, tq, tz, tabs,
-           send_sem, recv_own, recv_sib, tsend, trecv, local_sem):
+def kernel(tile_ref, v_ref, o_ref, xbuf, hi, lo, sq, ob, tq, tz, tabs,
+           send_sem, recv_own, recv_sib, tsend, trecv, local_sem, own_sem, out_sem):
     z = lax.axis_index("panel")
     x = lax.axis_index("layer")
     c = lax.axis_index("sub")
     xo, co = 1 - x, 1 - c
     rows, half, blk, _ = v_ref.shape
     slots = 2 * half
+    part = half // 2
     zero_block = hi.shape[0] - 1
 
     far = z // 2
@@ -66,22 +67,25 @@
         pl.semaphore_signal(barrier, inc=1, device_id=dev, device_id_type=MESH)
     pl.semaphore_wait(barrier, 5)
 
-    def piece(zz, xx, cc, r):
-        return xbuf.at[(zz * 2 + cc) * rows + r, pl.ds(xx * half, half)]
-
-    def number(zz, xx, r):
-        return (zz * 2 + xx) * rows + r
+    def piece(zz, xx, cc, r, h):
+        return xbuf.at[(zz * 2 + cc) * rows + r, pl.ds(xx * half + h * part, part)]
+
+    def number(zz, xx, r, h):
+        return ((zz * 2 + xx) * rows + r) * 2 + h
 
     sends = []
 
-    def send(pred, src, zz, xx, r, dev, sib=False):
+    def both(p, q):
+        return q if p is None else p if q is None else p & q
+
+    def send(pred, src, zz, xx, r, h, dev, sib=False):
         slot = len(sends)
         recv = recv_sib if sib else recv_own
         copy = pltpu.make_async_remote_copy(
             src_ref=src,
-            dst_ref=piece(zz, xx, c, r),
+            dst_ref=piece(zz, xx, c, r, h),
             send_sem=send_sem.at[slot],
-            recv_sem=recv.at[number(zz, xx, r)],
+            recv_sem=recv.at[number(zz, xx, r, h)],
             device_id=dev,
             device_id_type=MESH,
         )
@@ -91,13 +95,17 @@
         else:
             pl.when(pred)(copy.start)
 
-    def wait_piece(zz, xx, cc, r, sem):
-        dst = piece(zz, xx, cc, r)
-        pltpu.make_async_remote_copy(
+    def wait_piece(zz, xx, cc, r, h, sem, pred=None):
+        dst = piece(zz, xx, cc, r, h)
+        copy = pltpu.make_async_remote_copy(
             src_ref=dst, dst_ref=dst, send_sem=send_sem.at[0],
-            recv_sem=sem.at[number(zz, xx, r)],
+            recv_sem=sem.at[number(zz, xx, r, h)],
             device_id={"sub": co}, device_id_type=MESH,
-        ).wait_recv()
+        )
+        if pred is None:
+            copy.wait_recv()
+        else:
+            pl.when(pred)(copy.wait_recv)
 
     def small(src, dst, s, r, dev):
         return pltpu.make_async_remote_copy(
@@ -105,23 +113,27 @@
             device_id=dev, device_id_type=MESH,
         )
 
-    tq[x, c] = tile_ref[...]
-    t1 = small(tq.at[x, c], tq.at[x, c], 0, 0, {"sub": co})
-    t1.start()
-
+    own = []
     for r in range(rows):
-        own = v_ref.at[r]
-        send(None, own, z, x, r, {"panel": z_in})
-        send(is_mid, own, z, x, r, {"panel": z_out})
-        send(None, own, z, x, r, {"layer": xo})
-        send(None, own, z, x, r, {"sub": co}, sib=True)
+        for h in range(2):
+            src = v_ref.at[r, pl.ds(h * part, part)]
+            send(None, src, z, x, r, h, {"panel": z_in})
+            send(is_mid, src, z, x, r, h, {"panel": z_out})
+            send(None, src, z, x, r, h, {"layer": xo})
+            send(None, src, z, x, r, h, {"sub": co}, sib=True)
+            if r == 0 and h == 0:
+                tq[x, c] = tile_ref[...]
+                t1 = small(tq.at[x, c], tq.at[x, c], 0, 0, {"sub": co})
+                t1.start()
+    for r in range(rows):
+        own.append(pltpu.make_async_copy(
+            v_ref.at[r], xbuf.at[(z * 2 + c) * rows + r, pl.ds(x * half, half)], own_sem.at[r]))
+        own[r].start()
 
     t1.wait_recv()
     t2 = small(tq.at[x], tq.at[x], 1, 1, {"layer": xo})
     t2.start()
 
-    for r in range(rows):
-        xbuf[(z * 2 + c) * rows + r, pl.ds(x * half, half)] = v_ref[r]
     hi[zero_block] = jnp.zeros((blk, blk), jnp.bfloat16)
     lo[zero_block] = jnp.zeros((blk, blk), jnp.bfloat16)
     sq[...] = jnp.zeros_like(sq)
@@ -134,29 +146,39 @@
     for t in t3:
         t.start()
 
-    def arrive(q, other, r):
+    def arrive(q, other, r, h, pred=None):
         zz = q_list[q]
-        if not other:
-            wait_piece(zz, x, c, r, recv_own)
-            src = piece(zz, x, c, r)
-            if q == 1:
-                send(is_mid, src, zz, x, r, {"panel": z_in})
-                if r == 0:
-                    send(is_end, src, zz, x, r, {"layer": xo})
-            else:
-                send(is_mid, src, zz, x, r, {"panel": z_out})
-                send(None, src, zz, x, r, {"layer": xo})
-            send(None, src, zz, x, r, {"sub": co}, sib=True)
+        xx = xo if other else x
+        wait_piece(zz, xx, c, r, h, recv_own, pred)
+        src = piece(zz, xx, c, r, h)
+
+        def pass_on(p, dev, sib=False):
+            if p is None or pred is None or p is not pred:
+                p = both(p, pred)
+            send(p, src, zz, xx, r, h, dev, sib)
+
+        if other:
+            if q == 0:
+                pass_on(is_end, {"panel": z_in})
+        elif q == 1:
+            pass_on(is_mid, {"panel": z_in})
+            if r == 0:
+                pass_on(is_end, {"layer": xo})
         else:
-            wait_piece(zz, xo, c, r, recv_own)
-            src = piece(zz, xo, c, r)
-            if q == 0:
-                send(is_end, src, zz, xo, r, {"panel": z_in})
-            send(None, src, zz, xo, r, {"sub": co}, sib=True)
+            if pred is not is_end:
+                pass_on(is_mid, {"panel": z_out})
+            pass_on(None, {"layer": xo})
+        pass_on(None, {"sub": co}, sib=True)
+
+    def group(*pieces, pred=None):
+        for h in range(2):
+            for q, other, r in pieces:
+                arrive(q, other, r, h, pred)
 
     def late_extra():
         r = rows - 1
-        send(is_mid, piece(z, xo, c, r), z, xo, r, {"panel": z_out})
+        for h in range(2):
+            send(is_mid, piece(z, xo, c, r, h), z, xo, r, h, {"panel": z_out})
 
     def convert(row):
         val = xbuf[row]
@@ -172,74 +194,76 @@
     def chunk_ready(q, r):
         zz = q_list[q]
         for xx in (x, xo):
-            wait_piece(zz, xx, co, r, recv_sib)
+            for h in range(2):
+                wait_piece(zz, xx, co, r, h, recv_sib)
         for cc in range(2):
             convert((zz * 2 + cc) * rows + r)
 
     def times(lh, ll, wh, wl):
         m = lh.shape[0]
-        both = jnp.dot(jnp.concatenate([lh, ll], axis=0), wh, preferred_element_type=jnp.float32)
-        return both[:m] + both[m:] + jnp.dot(lh, wl, preferred_element_type=jnp.float32)
-
-    def chunk(q, r):
-        zz = q_list[q]
+        top = jnp.dot(jnp.concatenate([lh, ll], axis=0), wh, preferred_element_type=jnp.float32)
+        return top[:m] + top[m:] + jnp.dot(lh, wl, preferred_element_type=jnp.float32)
+
+    def chunk(*parts):
+        from_rows = [(q_list[q], cc, r) for q, r in parts for cc in range(2)]
 
         def one_row(i, carry):
-            lidx = [block_at(z, c, i, (zz * 2 + cc) * rows + r) for cc in range(2)]
+            lidx = [block_at(z, c, i, (zz * 2 + cc) * rows + r) for zz, cc, r in from_rows]
             lh = jnp.concatenate([hi[n] for n in lidx], axis=1)
             ll = jnp.concatenate([lo[n] for n in lidx], axis=1)
             for tp in range(slots // 2):
-                ridx = [
-                    [block_at(zz, cc, r, tabs[z, c, 2 + i, 2 * tp + e]) for cc in range(2)]
-                    for e in range(2)
-                ]
+                cols = [tabs[z, c, 2 + i, 2 * tp + e] for e in range(2)]
+                ridx = [[block_at(*row, col) for row in from_rows] for col in cols]
                 wh = jnp.concatenate(
-                    [jnp.concatenate([hi[n] for n in col], axis=0) for col in ridx], axis=1)
+                    [jnp.concatenate([hi[n] for n in one], axis=0) for one in ridx], axis=1)
                 wl = jnp.concatenate(
-                    [jnp.concatenate([lo[n] for n in col], axis=0) for col in ridx], axis=1)
+                    [jnp.concatenate([lo[n] for n in one], axis=0) for one in ridx], axis=1)
                 sq[i, tp] += times(lh, ll, wh, wl)
             return carry
 
         lax.fori_loop(0, rows, one_row, 0)
 
-    arrive(1, False, 0)
-    arrive(0, True, 0)
-    arrive(1, False, 1)
-    arrive(0, True, 1)
-    for zz, s in zip(others, range(3)):
+    group((1, False, 0), (0, True, 0))
+    group((2, False, 0), pred=is_mid)
+    group((1, False, 1), (0, True, 1))
+    group((2, False, 1), pred=is_mid)
+    for zz in others:
         small(tz.at[zz], tz.at[zz], 2, 2 + zz, {"sub": co}).wait_recv()
     stage = pltpu.make_async_copy(tz, tabs, local_sem)
     stage.start()
+    for r in range(rows):
+        own[r].wait()
     chunk_ready(0, 0)
     chunk_ready(0, 1)
     stage.wait()
-    chunk(0, 0)
-    arrive(2, False, 0)
-    arrive(2, False, 1)
-    chunk(0, 1)
-    arrive(1, True, 0)
+    group((2, False, 0), pred=is_end)
+    chunk((0, 0), (0, 1))
+    group((1, True, 0))
+    group((3, False, 0), pred=is_mid)
+    group((2, False, 1), pred=is_end)
     chunk_ready(1, 0)
-    chunk(1, 0)
-    arrive(2, True, 0)
+    chunk((1, 0))
+    group((2, True, 0))
+    group((3, False, 1), pred=is_mid)
+    late_extra()
+    group((3, False, 0), pred=is_end)
     chunk_ready(2, 0)
-    arrive(3, False, 0)
-    chunk(2, 0)
-    arrive(2, True, 1)
+    chunk((2, 0))
+    group((2, True, 1))
+    group((3, False, 1), pred=is_end)
+    group((1, True, 1), pred=is_mid)
     chunk_ready(2, 1)
-    arrive(3, False, 1)
-    late_extra()
-    chunk(2, 1)
-    arrive(3, True, 0)
+    chunk((2, 1))
+    group((3, True, 0))
     chunk_ready(3, 0)
-    chunk(3, 0)
-    arrive(3, True, 1)
-    arrive(1, True, 1)
+    chunk((3, 0))
+    group((1, True, 1), pred=is_end)
+    group((3, True, 1))
+    chunk_ready(1, 1)
     chunk_ready(3, 1)
-    chunk(3, 1)
-    chunk_ready(1, 1)
-    chunk(1, 1)
-
-    def cube_row(i, carry):
+    chunk((3, 1), (1, 1))
+
+    def cube_row(i):
         full = jnp.concatenate([sq[i, tp] for tp in range(slots // 2)], axis=1)
         sh = full.astype(jnp.bfloat16)
         sl = (full - sh.astype(jnp.float32)).astype(jnp.bfloat16)
@@ -258,11 +282,14 @@
             wl = jnp.concatenate(
                 [jnp.concatenate([lo[n] for n in one], axis=0) for one in idx], axis=1)
             res = 3.0 * sq[i, x * (half // 2) + e] - 2.0 * times(sh, sl, wh, wl)
-            o_ref[i, 2 * e] = res[:, :blk]
-            o_ref[i, 2 * e + 1] = res[:, blk:]
-        return carry
-
-    lax.fori_loop(0, rows, cube_row, 0)
+            ob[i, 2 * e] = res[:, :blk]
+            ob[i, 2 * e + 1] = res[:, blk:]
+
+    outs = []
+    for i in range(rows):
+        cube_row(i)
+        outs.append(pltpu.make_async_copy(ob.at[i], o_ref.at[i], out_sem.at[i]))
+        outs[i].start()
 
     for t in (t1, t2, *t3):
         t.wait_send()
@@ -271,6 +298,8 @@
             copy.wait_send()
         else:
             pl.when(pred)(copy.wait_send)
+    for i in range(rows):
+        outs[i].wait()
 
 
 def shards_kernel(values, columns):
@@ -289,22 +318,25 @@
     return pl.pallas_call(
         kernel,
         out_shape=jax.ShapeDtypeStruct(values.shape, jnp.float32),
-        in_specs=[vmem, vmem],
-        out_specs=vmem,
+        in_specs=[vmem, pl.BlockSpec(memory_space=pl.ANY)],
+        out_specs=pl.BlockSpec(memory_space=pl.ANY),
         scratch_shapes=[
             pltpu.VMEM((nb, slots, blk, blk), jnp.float32),
             pltpu.VMEM((nb * slots + 1, blk, blk), jnp.bfloat16),
             pltpu.VMEM((nb * slots + 1, blk, blk), jnp.bfloat16),
             pltpu.VMEM((rows, slots // 2, blk, 2 * blk), jnp.float32),
+            pltpu.VMEM(values.shape, jnp.float32),
             pltpu.VMEM((2, 2, 8, 128), jnp.int32),
             pltpu.VMEM((4, 2, 8, 128), jnp.int32),
             pltpu.SMEM((4, 2, 8, 128), jnp.int32),
-            pltpu.SemaphoreType.DMA((36,)),
-            pltpu.SemaphoreType.DMA((4 * 2 * rows,)),
-            pltpu.SemaphoreType.DMA((4 * 2 * rows,)),
+            pltpu.SemaphoreType.DMA((96,)),
+            pltpu.SemaphoreType.DMA((4 * 2 * rows * 2,)),
+            pltpu.SemaphoreType.DMA((4 * 2 * rows * 2,)),
             pltpu.SemaphoreType.DMA((5,)),
             pltpu.SemaphoreType.DMA((6,)),
             pltpu.SemaphoreType.DMA,
+            pltpu.SemaphoreType.DMA((rows,)),
+            pltpu.SemaphoreType.DMA((rows,)),
         ],
         compiler_params=pltpu.CompilerParams(
             collective_id=0, has_side_effects=True, vmem_limit_bytes=48 * 1024 * 1024,

time: 60.8 us -> 55.8 us (0.918)
  Pallas kernels: 57.9 us -> 52.4 us
    pallas_call x1, Pallas kernels: 57.9 us -> 52.4 us  [shards_kernel(): pl.pallas_call(kernel, out_shape=jax.ShapeDtypeStruct(values.shape, jnp.f...]
where the time goes in v2:
time: 55.8 us; the launch traced here: 55.2 us
  Pallas kernels  52.4 us (94%)
  local copies, waits for them, and re-layouts  2.52 us (5%)
    pallas_call x1, Pallas kernels, shards_kernel(): pl.pallas_call(kernel, out_shape=jax.ShapeDtypeStruct(values.shape, jnp.f...  52.4 us
    unnamed x5, local copies, waits for them, and re-layouts  2.44 us

profile of v2, /device:TPU:0, one launch (start us, length us, event | category | flops | bytes accessed | tf_op | source)
XLA Modules:
  0.0 55.2 jit_solution(14700188220741250835)
XLA Ops:
  0.0 0.1 pad.2.clone
  0.1 0.0 copy-start.1
  0.1 0.1 iota_compare_fusion.1
  0.2 0.6 %copy-done.1 = s32[2,4]{1,0:T(2,128)S(1)} copy-done((s32[2,4]{1,0:T(2,128)S(1)}, s32[2,4]{1,0:T(2,128)}, u32[]{:S(2)}) %copy-start.1) | copy-done | bytes 56
  0.8 0.1 select_reduce_fusion.1
  0.9 0.1 add_add_fusion.tile_ref
  0.9 0.0 copy-start
  0.9 1.0 %copy-done = f32[2,4,128,128]{3,2,1,0:T(8,128)S(1)} copy-done((f32[2,4,128,128]{3,2,1,0:T(8,128)S(1)}, f32[2,4,128,128]{3,2,1,0:T(8,128)}, u32[]{:S(2)}) %copy-start) | copy-done | bytes 524312
  2.0 52.4 %shard_map.28 = f32[2,4,128,128]{3,2,1,0:T(8,128)S(1)} custom-call(s32[8,128]{1,0:T(8,128)S(1)} %add_add_fusion.tile_ref, f32[2,4,128,128]{3,2,1,0:T(8,128)S(1)} %copy-done), custom_call_target="tpu_custom_call" | custom-call | flops 4831838208 | bytes 1048576 | tf_op jit(solution)/shard_map/pallas_call | solution.py:318
  54.4 0.8 %copy.4 = f32[2,4,128,128]{3,2,1,0:T(8,128)} copy(f32[2,4,128,128]{3,2,1,0:T(8,128)S(1)} %shard_map.28) | data formatting | bytes 1048576
  (2 shorter events, 0.0 us)
Async XLA Ops:
  0.1 0.7 %copy-start.1 = (s32[2,4]{1,0:T(2,128)S(1)}, s32[2,4]{1,0:T(2,128)}, u32[]{:S(2)}) copy-start(s32[2,4]{1,0:T(2,128)} %param.3) | copy-start | bytes 100
  0.9 1.0 %copy-start = (f32[2,4,128,128]{3,2,1,0:T(8,128)S(1)}, f32[2,4,128,128]{3,2,1,0:T(8,128)}, u32[]{:S(2)}) copy-start(f32[2,4,128,128]{3,2,1,0:T(8,128)} %v_ref.1) | copy-start | bytes 1572868

commit v3 on v2

--- a/solution.py
+++ b/solution.py
@@ -38,8 +38,8 @@
     return 3.0 * square_own - 2.0 * cube_own
 
 
-def kernel(tile_ref, v_ref, o_ref, xbuf, hi, lo, sq, ob, tq, tz, tabs,
-           send_sem, recv_own, recv_sib, tsend, trecv, local_sem, own_sem, out_sem):
+def kernel(cols_ref, v_ref, o_ref, xbuf, hi, lo, sq, tq, tz, tabs,
+           send_sem, recv_own, recv_sib, tsend, trecv, local_sem, own_sem):
     z = lax.axis_index("panel")
     x = lax.axis_index("layer")
     c = lax.axis_index("sub")
@@ -75,17 +75,34 @@
 
     sends = []
 
+    def row_piece(zz, xx, cc, r):
+        return xbuf.at[(zz * 2 + cc) * rows + r, pl.ds(xx * half, half)]
+
+    def send_sib(pred, src, zz, xx, r):
+        copy = pltpu.make_async_remote_copy(
+            src_ref=src,
+            dst_ref=row_piece(zz, xx, c, r),
+            send_sem=send_sem.at[len(sends)],
+            recv_sem=recv_sib.at[(zz * 2 + xx) * rows + r],
+            device_id={"sub": co},
+            device_id_type=MESH,
+        )
+        sends.append((pred, copy))
+        if pred is None:
+            copy.start()
+        else:
+            pl.when(pred)(copy.start)
+
     def both(p, q):
         return q if p is None else p if q is None else p & q
 
-    def send(pred, src, zz, xx, r, h, dev, sib=False):
+    def send(pred, src, zz, xx, r, h, dev):
         slot = len(sends)
-        recv = recv_sib if sib else recv_own
         copy = pltpu.make_async_remote_copy(
             src_ref=src,
             dst_ref=piece(zz, xx, c, r, h),
             send_sem=send_sem.at[slot],
-            recv_sem=recv.at[number(zz, xx, r, h)],
+            recv_sem=recv_own.at[number(zz, xx, r, h)],
             device_id=dev,
             device_id_type=MESH,
         )
@@ -95,11 +112,11 @@
         else:
             pl.when(pred)(copy.start)
 
-    def wait_piece(zz, xx, cc, r, h, sem, pred=None):
-        dst = piece(zz, xx, cc, r, h)
+    def wait_piece(zz, xx, r, h, pred=None):
+        dst = piece(zz, xx, c, r, h)
         copy = pltpu.make_async_remote_copy(
             src_ref=dst, dst_ref=dst, send_sem=send_sem.at[0],
-            recv_sem=sem.at[number(zz, xx, r, h)],
+            recv_sem=recv_own.at[number(zz, xx, r, h)],
             device_id={"sub": co}, device_id_type=MESH,
         )
         if pred is None:
@@ -120,16 +137,25 @@
             send(None, src, z, x, r, h, {"panel": z_in})
             send(is_mid, src, z, x, r, h, {"panel": z_out})
             send(None, src, z, x, r, h, {"layer": xo})
-            send(None, src, z, x, r, h, {"sub": co}, sib=True)
-            if r == 0 and h == 0:
-                tq[x, c] = tile_ref[...]
-                t1 = small(tq.at[x, c], tq.at[x, c], 0, 0, {"sub": co})
-                t1.start()
     for r in range(rows):
+        send_sib(None, v_ref.at[r], z, x, r)
         own.append(pltpu.make_async_copy(
             v_ref.at[r], xbuf.at[(z * 2 + c) * rows + r, pl.ds(x * half, half)], own_sem.at[r]))
         own[r].start()
 
+    cols = cols_ref[...]
+    lanes = lax.broadcasted_iota(jnp.int32, (rows, 128), 1)
+    by_col = jnp.zeros((rows, 128), jnp.int32)
+    by_slot = jnp.zeros((rows, 128), jnp.int32)
+    for s in range(half):
+        col = cols[:, s:s + 1]
+        by_col = jnp.where(col == lanes, x * half + s + 1, by_col)
+        by_slot = jnp.where(lanes == x * half + s, col, by_slot)
+    rest = jnp.zeros((8 - 2 * rows, 128), jnp.int32)
+    tq[x, c] = jnp.concatenate([by_col, by_slot, rest], axis=0)
+    t1 = small(tq.at[x, c], tq.at[x, c], 0, 0, {"sub": co})
+    t1.start()
+
     t1.wait_recv()
     t2 = small(tq.at[x], tq.at[x], 1, 1, {"layer": xo})
     t2.start()
@@ -139,7 +165,7 @@
     sq[...] = jnp.zeros_like(sq)
 
     t2.wait_recv()
-    tz[z] = tq[0] + tq[1]
+    tz[z] = jnp.maximum(tq[0], tq[1])
     t3 = [
         small(tz.at[z], tz.at[z], 2 + d, 2 + z, {"panel": others[d]}) for d in range(3)
     ]
@@ -149,13 +175,13 @@
     def arrive(q, other, r, h, pred=None):
         zz = q_list[q]
         xx = xo if other else x
-        wait_piece(zz, xx, c, r, h, recv_own, pred)
+        wait_piece(zz, xx, r, h, pred)
         src = piece(zz, xx, c, r, h)
 
-        def pass_on(p, dev, sib=False):
+        def pass_on(p, dev):
             if p is None or pred is None or p is not pred:
                 p = both(p, pred)
-            send(p, src, zz, xx, r, h, dev, sib)
+            send(p, src, zz, xx, r, h, dev)
 
         if other:
             if q == 0:
@@ -168,7 +194,8 @@
             if pred is not is_end:
                 pass_on(is_mid, {"panel": z_out})
             pass_on(None, {"layer": xo})
-        pass_on(None, {"sub": co}, sib=True)
+        if h == 1:
+            send_sib(pred, row_piece(zz, xx, c, r), zz, xx, r)
 
     def group(*pieces, pred=None):
         for h in range(2):
@@ -194,8 +221,12 @@
     def chunk_ready(q, r):
         zz = q_list[q]
         for xx in (x, xo):
-            for h in range(2):
-                wait_piece(zz, xx, co, r, h, recv_sib)
+            dst = row_piece(zz, xx, co, r)
+            pltpu.make_async_remote_copy(
+                src_ref=dst, dst_ref=dst, send_sem=send_sem.at[0],
+                recv_sem=recv_sib.at[(zz * 2 + xx) * rows + r],
+                device_id={"sub": co}, device_id_type=MESH,
+            ).wait_recv()
         for cc in range(2):
             convert((zz * 2 + cc) * rows + r)
 
@@ -282,14 +313,11 @@
             wl = jnp.concatenate(
                 [jnp.concatenate([lo[n] for n in one], axis=0) for one in idx], axis=1)
             res = 3.0 * sq[i, x * (half // 2) + e] - 2.0 * times(sh, sl, wh, wl)
-            ob[i, 2 * e] = res[:, :blk]
-            ob[i, 2 * e + 1] = res[:, blk:]
-
-    outs = []
+            o_ref[i, 2 * e] = res[:, :blk]
+            o_ref[i, 2 * e + 1] = res[:, blk:]
+
     for i in range(rows):
         cube_row(i)
-        outs.append(pltpu.make_async_copy(ob.at[i], o_ref.at[i], out_sem.at[i]))
-        outs[i].start()
 
     for t in (t1, t2, *t3):
         t.wait_send()
@@ -298,34 +326,24 @@
             copy.wait_send()
         else:
             pl.when(pred)(copy.wait_send)
-    for i in range(rows):
-        outs[i].wait()
 
 
 def shards_kernel(values, columns):
     rows, half, blk, _ = values.shape
     slots, nb = 2 * half, 8 * rows
-    x = lax.axis_index("layer")
-    lanes = jnp.arange(128, dtype=jnp.int32)
-    place = jnp.arange(half, dtype=jnp.int32) + x * half
-    by_col = jnp.sum(
-        jnp.where(columns[:, :, None] == lanes, place[None, :, None] + 1, 0), axis=1)
-    by_slot = jnp.sum(
-        jnp.where(place[None, :, None] == lanes, columns[:, :, None], 0), axis=1)
-    tile = jnp.concatenate(
-        [by_col, by_slot, jnp.zeros((8 - 2 * rows, 128), jnp.int32)], axis=0).astype(jnp.int32)
-    vmem = pl.BlockSpec(memory_space=pltpu.VMEM)
     return pl.pallas_call(
         kernel,
         out_shape=jax.ShapeDtypeStruct(values.shape, jnp.float32),
-        in_specs=[vmem, pl.BlockSpec(memory_space=pl.ANY)],
-        out_specs=pl.BlockSpec(memory_space=pl.ANY),
+        in_specs=[
+            pl.BlockSpec(memory_space=pltpu.VMEM),
+            pl.BlockSpec(memory_space=pltpu.HBM),
+        ],
+        out_specs=pl.BlockSpec(memory_space=pltpu.VMEM),
         scratch_shapes=[
             pltpu.VMEM((nb, slots, blk, blk), jnp.float32),
             pltpu.VMEM((nb * slots + 1, blk, blk), jnp.bfloat16),
             pltpu.VMEM((nb * slots + 1, blk, blk), jnp.bfloat16),
             pltpu.VMEM((rows, slots // 2, blk, 2 * blk), jnp.float32),
-            pltpu.VMEM(values.shape, jnp.float32),
             pltpu.VMEM((2, 2, 8, 128), jnp.int32),
             pltpu.VMEM((4, 2, 8, 128), jnp.int32),
             pltpu.SMEM((4, 2, 8, 128), jnp.int32),
@@ -336,7 +354,6 @@
             pltpu.SemaphoreType.DMA((6,)),
             pltpu.SemaphoreType.DMA,
             pltpu.SemaphoreType.DMA((rows,)),
-            pltpu.SemaphoreType.DMA((rows,)),
         ],
         compiler_params=pltpu.CompilerParams(
             collective_id=0, has_side_effects=True, vmem_limit_bytes=48 * 1024 * 1024,
@@ -344,7 +361,7 @@
         cost_estimate=pl.CostEstimate(
             flops=3 * 2 * 3 * 64 * 2 * blk ** 3, bytes_accessed=2 * values.size * 4,
             transcendentals=0),
-    )(tile, values)
+    )(columns, values)
 
 
 def solution(mesh):

time: 55.8 us -> 55.5 us (level)
  no operation moved by 1% of the time
where the time goes in v3:
time: 55.5 us; the launch traced here: 54.6 us
  Pallas kernels  52.1 us (94%)
  local copies, waits for them, and re-layouts  2.52 us (5%)
    pallas_call x1, Pallas kernels, shards_kernel(): pl.pallas_call(kernel, out_shape=jax.ShapeDtypeStruct(values.shape, jnp.f...  52.1 us
    unnamed x5, local copies, waits for them, and re-layouts  2.52 us

profile of v3, /device:TPU:0, one launch (start us, length us, event | category | flops | bytes accessed | tf_op | source)
XLA Modules:
  0.0 54.6 jit_solution(15191837951576542009)
XLA Ops:
  0.0 0.0 copy-start
  0.0 1.0 %copy-done = f32[2,4,128,128]{3,2,1,0:T(8,128)S(1)} copy-done((f32[2,4,128,128]{3,2,1,0:T(8,128)S(1)}, f32[2,4,128,128]{3,2,1,0:T(8,128)}, u32[]{:S(2)}) %copy-start) | copy-done | bytes 524312
  1.0 0.0 copy-start.1
  1.0 0.7 %copy-done.1 = s32[2,4]{1,0:T(2,128)S(1)} copy-done((s32[2,4]{1,0:T(2,128)S(1)}, s32[2,4]{1,0:T(2,128)}, u32[]{:S(2)}) %copy-start.1) | copy-done | bytes 56
  1.7 52.1 %shard_map.28 = f32[2,4,128,128]{3,2,1,0:T(8,128)S(1)} custom-call(s32[2,4]{1,0:T(2,128)S(1)} %copy-done.1, f32[2,4,128,128]{3,2,1,0:T(8,128)S(1)} %copy-done), custom_call_target="tpu_custom_call" | custom-call | flops 4831838208 | bytes 1048576 | tf_op jit(solution)/shard_map/pallas_call | solution.py:334
  53.8 0.8 %copy.4 = f32[2,4,128,128]{3,2,1,0:T(8,128)} copy(f32[2,4,128,128]{3,2,1,0:T(8,128)S(1)} %shard_map.28) | data formatting | bytes 1048576
Async XLA Ops:
  0.0 1.0 %copy-start = (f32[2,4,128,128]{3,2,1,0:T(8,128)S(1)}, f32[2,4,128,128]{3,2,1,0:T(8,128)}, u32[]{:S(2)}) copy-start(f32[2,4,128,128]{3,2,1,0:T(8,128)} %v_ref.1) | copy-start | bytes 1572868
  1.0 0.7 %copy-start.1 = (s32[2,4]{1,0:T(2,128)S(1)}, s32[2,4]{1,0:T(2,128)}, u32[]{:S(2)}) copy-start(s32[2,4]{1,0:T(2,128)} %cols_ref.1) | copy-start | bytes 100
